TPU v7x, 512 devices: a whole 4x8x8 slice. The times are simulated.
512 devices in a mesh: hours: 64 (over z, x, core), region: 8 (over y).
Axes of the slice: x: 4, y: 8, z: 8, core: 2. Of those that a mesh axis runs over, the one named last changes fastest.
Arguments:
- availability: float32 [4096, 16, 1024], P('hours', None, 'region'), may hold values from 0.1 to 1
- demand: float32 [4096, 1024], P('hours', 'region'), may hold values from 2 to 72, as said below
- gen_cost: float32 [16, 1024], P(None, 'region'), may hold values from 0.05 to 1
- cap_cost: float32 [8, 2048], P('region', 'hours'), may hold values from 204.8 to 2048
- owner_map: int32 [8, 2048], P('region'), may hold values from 0 to 2047, each once within a row
- line_ends: int32 [2, 2048], P(None, 'region'), may hold values from 0 to 127
- line_limit: float32 [2048], P('region'), may hold values from 0.5 to 4
- cross_ends: int32 [2, 8, 256], P(None, 'region'), may hold values from 0 to 127
- cross_limit: float32 [8, 256], P('region'), may hold values from 0.5 to 4
- pair_counts: int32 [8, 8], P('region'), may hold values from 0 to 32, as said below
- store_node: int32 [2048], P('region'), may hold values from 0 to 127
- store_energy: float32 [2048], P('region'), may hold values from 0.02 to 0.4
- store_power: float32 [2048], P('region'), may hold values from 0.2 to 2
- price_start: float32 [4096, 1024], P('hours', 'region'), may hold values from -3 to 0.5
Outputs:
- dispatch: float32 [4096, 16, 1024], P('hours', None, 'region')
- capacity: float32 [8, 2048], P('region', 'hours')
- prices: float32 [4096, 1024], P('hours', 'region')
- charge_state: float32 [4096, 2048], P('hours', 'region')
Inputs may be any that keep to these rules, and one draw needn't show every extreme that they name: `demand`: loads are positive. `owner_map`: each row lists every capacity column of its region once. `pair_counts`: cross lines in use among the 32 slots of each ordered pair of regions; a region has none to itself; some pair uses all 32.
All inputs are finite; a program needn't handle non-finite values.
Results may differ from a plain program's by a relative error of at most 0.00018.
Values sent between devices are 32-bit elements; how exact they have to be, the bound alone decides.
A program may use at most 64 MiB of HBM per device.

v0:
```python
import jax
import jax.numpy as jnp
from jax import lax
from jax.sharding import PartitionSpec as P

ITERS = 4
epsilon = 1e-06
highest = lax.Precision.HIGHEST


def shifted(value, axis, steps):
    count = lax.axis_size(axis)
    pairs = [(source, (source + steps) % count) for source in range(count)]
    return lax.ppermute(value, axis, pairs)


def one_hot(indices, labels):
    return (indices[:, None] == labels[None, :]).astype(jnp.float32)


def to_owners(partial_value, owned_cols):
    summed = lax.psum(partial_value, "hours")
    return lax.dynamic_slice_in_dim(summed, lax.axis_index("hours") * owned_cols, owned_cols)


def spread_columns(capacity_bar):
    return lax.all_gather(capacity_bar, "hours", axis=0, tiled=True)


def body(
    availability,
    demand,
    gen_cost,
    cap_cost,
    owner_map,
    line_ends,
    line_limit,
    cross_ends,
    cross_limit,
    pair_counts,
    store_node,
    store_energy,
    store_power,
    price_start,
):
    hour_rows, tech_count, node_count = availability.shape
    region_count = lax.axis_size("region")
    slot_count = cross_limit.shape[1]
    slot_width = slot_count // region_count
    owned_cols = cap_cost.shape[1]
    owner_cols = owner_map[0]
    inverse = jnp.argsort(owner_cols)
    node_ids = jnp.arange(node_count, dtype=jnp.int32)
    line_inc = one_hot(line_ends[1], node_ids) - one_hot(line_ends[0], node_ids)
    store_map = one_hot(store_node, node_ids)
    leave_map = one_hot(cross_ends[0, 0], node_ids)
    slot_ids = jnp.arange(slot_count, dtype=jnp.int32)
    pair_of = slot_ids // slot_width
    region_ids = jnp.arange(region_count, dtype=jnp.int32)
    in_use = jnp.sum(
        jnp.where(pair_of[:, None] == region_ids[None, :], pair_counts[0][None, :], 0), axis=1
    )
    cross_bound = jnp.where(slot_ids % slot_width < in_use, cross_limit[0], 0.0)
    reach_map = one_hot(
        pair_of * node_count + cross_ends[1, 0],
        jnp.arange(region_count * node_count, dtype=jnp.int32),
    )
    column_costs = cap_cost[0]
    col_weight = to_owners(jnp.sum(availability, axis=0).reshape(-1)[owner_cols], owned_cols)
    dispatch = jnp.zeros_like(availability)
    capacity = jnp.zeros((owned_cols,), jnp.float32)
    inner_flow = jnp.zeros((hour_rows, line_limit.shape[0]), jnp.float32)
    cross_flow = jnp.zeros((hour_rows, slot_count), jnp.float32)
    mirror_flow = jnp.zeros((hour_rows, slot_count), jnp.float32)
    discharge = jnp.zeros((hour_rows, store_node.shape[0]), jnp.float32)
    charge = jnp.zeros((hour_rows, store_node.shape[0]), jnp.float32)
    prices = price_start
    cap_duals = jnp.zeros_like(availability)
    store_duals = jnp.zeros((hour_rows, store_node.shape[0]), jnp.float32)
    weight = jnp.float32(1.0)
    for iteration in range(ITERS):
        final_sweep = iteration == ITERS - 1
        primal_step = 0.5 / weight
        far_side = jnp.dot(
            lax.all_gather(prices, "region", axis=1, tiled=True), reach_map.T, precision=highest
        )
        if iteration == 0:
            next_duals = jnp.zeros_like(store_duals)
            cap_pull = jnp.zeros((owned_cols,), jnp.float32)
        else:
            next_row = shifted(store_duals[:1], "hours", -1)
            next_duals = jnp.concatenate([store_duals[1:], next_row], axis=0)
            cap_pull = to_owners(
                jnp.sum(availability * cap_duals, axis=0).reshape(-1)[owner_cols], owned_cols
            )
        dispatch_new = jnp.maximum(
            dispatch - primal_step * (gen_cost[None] + prices[:, None, :] + cap_duals), 0.0
        )
        capacity_new = jnp.maximum(
            capacity - (column_costs - cap_pull) / (weight * col_weight), 0.0
        )
        inner_new = jnp.clip(
            inner_flow - primal_step * jnp.dot(prices, line_inc.T, precision=highest),
            -line_limit,
            line_limit,
        )
        cross_new = jnp.clip(
            cross_flow - primal_step * (far_side - jnp.dot(prices, leave_map.T, precision=highest)),
            -cross_bound,
            cross_bound,
        )
        mirror_new = mirror_flow
        discharge_new = jnp.clip(
            discharge
            - primal_step * (jnp.dot(prices, store_map.T, precision=highest) + store_duals),
            -store_power,
            store_power,
        )
        charge_new = jnp.clip(charge - primal_step * (store_duals - next_duals), 0.0, store_energy)
        if not final_sweep:
            cap_change = capacity_new - capacity
            primal_sq = (
                jnp.sum((dispatch_new - dispatch) ** 2)
                + jnp.sum(cap_change**2)
                + jnp.sum((inner_new - inner_flow) ** 2)
                + jnp.sum((cross_new - cross_flow) ** 2)
                + jnp.sum((discharge_new - discharge) ** 2)
                + jnp.sum((charge_new - charge) ** 2)
            )
            primal_sum = lax.psum(primal_sq, ("hours", "region"))
        dispatch_bar = 2.0 * dispatch_new - dispatch
        capacity_bar = 2.0 * capacity_new - capacity
        inner_bar = 2.0 * inner_new - inner_flow
        cross_bar = 2.0 * cross_new - cross_flow
        discharge_bar = 2.0 * discharge_new - discharge
        charge_bar = 2.0 * charge_new - charge
        capacity_all = spread_columns(capacity_bar)
        cap_dense = capacity_all[inverse].reshape(tech_count, node_count)
        per_dest = jnp.dot(cross_bar, reach_map, precision=highest)
        balance = (
            jnp.sum(dispatch_bar, axis=1)
            + jnp.dot(inner_bar, line_inc, precision=highest)
            + (
                lax.psum_scatter(per_dest, "region", scatter_dimension=1, tiled=True)
                - jnp.dot(cross_bar, leave_map, precision=highest)
            )
            + jnp.dot(discharge_bar, store_map, precision=highest)
            - demand
        )
        prev_row = shifted(charge_bar[-1:], "hours", 1)
        storage_rows = (
            charge_bar - jnp.concatenate([prev_row, charge_bar[:-1]], axis=0) + discharge_bar
        )
        cap_rows = dispatch_bar - availability * cap_dense[None]
        prices_new = prices + weight / (tech_count + 8.0) * balance
        cap_new = jnp.maximum(cap_duals + weight / 2.0 * cap_rows, 0.0)
        store_new = store_duals + weight / 3.0 * storage_rows
        if not final_sweep:
            dual_sq = (
                jnp.sum((prices_new - prices) ** 2)
                + jnp.sum((cap_new - cap_duals) ** 2)
                + jnp.sum((store_new - store_duals) ** 2)
            )
            dual_sum = lax.psum(dual_sq, ("hours", "region"))
            weight = jnp.sqrt(weight * jnp.sqrt((dual_sum + epsilon) / (primal_sum + epsilon)))
        dispatch, capacity, inner_flow, cross_flow = (
            dispatch_new,
            capacity_new,
            inner_new,
            cross_new,
        )
        mirror_flow = mirror_new
        discharge, charge = (discharge_new, charge_new)
        prices, cap_duals, store_duals = (prices_new, cap_new, store_new)
    return (dispatch, capacity[None], prices, charge)


def solution(mesh):
    placed = (
        P("hours", None, "region"),
        P("hours", "region"),
        P(None, "region"),
        P("region", "hours"),
        P("region", None),
        P(None, "region"),
        P("region"),
        P(None, "region", None),
        P("region", None),
        P("region", None),
        P("region"),
        P("region"),
        P("region"),
        P("hours", "region"),
    )
    return jax.shard_map(
        body,
        mesh=mesh,
        in_specs=placed,
        out_specs=(
            P("hours", None, "region"),
            P("region", "hours"),
            P("hours", "region"),
            P("hours", "region"),
        ),
        check_vma=False,
    )
```

profile of v0, /device:TPU:2, one launch (start us, length us, event | category | flops | bytes accessed | tf_op | source)
XLA Modules:
  0.0 1496.5 jit_solution(16780039333863139814)
XLA Ops:
  7.2 0.7 broadcast_minimum_fusion
  7.9 2.0 collective-permute-start
  10.0 26.6 %all_gather.21 = f32[64,1024]{1,0:T(8,128)S(1)} all-gather(f32[64,128]{1,0:T(8,128)} %param.27), channel_id=1, replica_groups=mesh['hours'=64,'region'=8] {'region'}, dimensions={1}, use_global_device_ids=true | all-gather | bytes 294912 | tf_op jit(solution)/shard_map/all_gather | solution.py:85
  37.3 0.7 fusion.75
  38.1 0.9 multiply_reduce_fusion.20
  39.0 1.3 fusion.74
  41.2 11.8 gather_fusion
  53.0 126.8 %psum.70 = f32[2048]{0:T(1024)S(1)} all-reduce(f32[2048]{0:T(1024)S(1)} %gather_fusion), channel_id=1, replica_groups=mesh['hours'=64,'region'=8] {'hours'}, use_global_device_ids=true, to_apply=%region_5.6 | all-reduce | flops 2048 | bytes 16384 | tf_op jit(solution)/shard_map/psum | solution.py:22
  179.7 1.3 dynamic-slice
  181.7 0.7 multiply_reduce_fusion.28
  182.5 126.4 %all-reduce = f32[2048]{0:T(1024)S(1)} all-reduce(f32[2048]{0:T(1024)S(1)} %multiply_dynamic-update-slice_fusion), channel_id=1, replica_groups=mesh['hours'=64,'region'=8] {'hours'}, use_global_device_ids=true, to_apply=%add | all-reduce | flops 2048 | bytes 16384
  308.9 5.0 sort.17
  314.0 11.8 gather_fusion.1
  325.8 1.1 multiply_reduce_fusion.6
  326.8 11.8 gather_fusion.2
  338.6 1.0 multiply_reduce_fusion.21
  339.6 0.7 broadcast_reduce_fusion
  340.6 126.1 %psum.73 = f32[2048]{0:T(1024)S(1)} all-reduce(f32[2048]{0:T(1024)S(1)} %gather_fusion.2), channel_id=1, replica_groups=mesh['hours'=64,'region'=8] {'hours'}, use_global_device_ids=true, to_apply=%region_21.22 | all-reduce | flops 2048 | bytes 16384 | tf_op jit(solution)/shard_map/psum | solution.py:22
  469.9 0.9 multiply_reduce_fusion.19
  472.2 1.0 fusion.67
  473.2 0.9 multiply_reduce_fusion.25
  476.0 7.0 collective-permute-start.1
  483.0 95.3 %all-reduce.5 = (f32[]{:T(128)}, f32[]{:T(128)}) all-reduce(f32[]{:T(128)S(6)} %add.309, f32[]{:T(128)S(6)} %add.315), channel_id=1, replica_groups=mesh['hours'=64,'region'=8] {'hours','region'}, use_global_device_ids=true, to_apply=%region_9.10 | all-reduce | flops 2 | bytes 16 | tf_op jit(solution)/shard_map/psum | solution.py:164
  579.7 24.8 %all_gather.23 = f32[64,1024]{1,0:T(8,128)S(1)} all-gather(f32[64,128]{1,0:T(8,128)S(1)} %get-tuple-element.56), channel_id=1, replica_groups=mesh['hours'=64,'region'=8] {'region'}, dimensions={1}, use_global_device_ids=true | all-gather | bytes 294912 | tf_op jit(solution)/shard_map/all_gather | solution.py:85
  604.5 1.0 multiply_reduce_fusion.17
  605.6 0.7 multiply_reduce_fusion.27
  606.4 120.4 %all-reduce.1 = f32[2048]{0:T(1024)S(1)} all-reduce(f32[2048]{0:T(1024)S(1)} %subtract_dynamic-update-slice_fusion.1), channel_id=1, replica_groups=mesh['hours'=64,'region'=8] {'hours'}, use_global_device_ids=true, to_apply=%add.1 | all-reduce | flops 2048 | bytes 16384
  726.8 11.8 gather_fusion.3
  739.9 0.7 fusion.73
  740.7 0.9 multiply_reduce_fusion.16
  741.6 1.3 fusion.72
  742.9 1.2 multiply_reduce_fusion.3
  744.2 11.8 gather_fusion.4
  756.0 1.9 collective-permute-start.2
  758.2 131.1 %psum.76 = f32[2048]{0:T(1024)S(1)} all-reduce(f32[2048]{0:T(1024)S(1)} %gather_fusion.4), channel_id=1, replica_groups=mesh['hours'=64,'region'=8] {'hours'}, use_global_device_ids=true, to_apply=%region_36.37 | all-reduce | flops 2048 | bytes 16384 | tf_op jit(solution)/shard_map/psum | solution.py:22
  891.9 1.0 multiply_reduce_fusion.15
  894.2 1.0 fusion.63
  895.2 0.9 multiply_reduce_fusion.24
  898.0 1.9 collective-permute-start.3
  900.0 100.8 %all-reduce.4 = (f32[]{:T(128)}, f32[]{:T(128)}) all-reduce(f32[]{:T(128)S(6)} %add.329, f32[]{:T(128)S(6)} %add.335), channel_id=1, replica_groups=mesh['hours'=64,'region'=8] {'hours','region'}, use_global_device_ids=true, to_apply=%region_24.25 | all-reduce | flops 2 | bytes 16 | tf_op jit(solution)/shard_map/psum | solution.py:164
  1002.2 0.7 multiply_reduce_fusion.26
  1002.9 1.0 multiply_reduce_fusion.12
  1003.9 24.8 %all_gather.25 = f32[64,1024]{1,0:T(8,128)S(1)} all-gather(f32[64,128]{1,0:T(8,128)S(1)} %get-tuple-element.63), channel_id=1, replica_groups=mesh['hours'=64,'region'=8] {'region'}, dimensions={1}, use_global_device_ids=true | all-gather | bytes 294912 | tf_op jit(solution)/shard_map/all_gather | solution.py:85
  1029.5 120.4 %all-reduce.2 = f32[2048]{0:T(1024)S(1)} all-reduce(f32[2048]{0:T(1024)S(1)} %subtract_dynamic-update-slice_fusion), channel_id=1, replica_groups=mesh['hours'=64,'region'=8] {'hours'}, use_global_device_ids=true, to_apply=%add.2 | all-reduce | flops 2048 | bytes 16384
  1149.9 11.8 gather_fusion.5
  1161.7 1.9 collective-permute-start.4
  1163.7 0.7 fusion.71
  1164.4 0.9 multiply_reduce_fusion.11
  1165.3 1.3 fusion.70
  1166.7 1.4 multiply_reduce_fusion
  1168.1 11.8 gather_fusion.6
  1180.2 131.1 %psum.79 = f32[2048]{0:T(1024)S(1)} all-reduce(f32[2048]{0:T(1024)S(1)} %gather_fusion.6), channel_id=1, replica_groups=mesh['hours'=64,'region'=8] {'hours'}, use_global_device_ids=true, to_apply=%region_48.49 | all-reduce | flops 2048 | bytes 16384 | tf_op jit(solution)/shard_map/psum | solution.py:22
  1313.9 0.9 multiply_reduce_fusion.13
  1316.2 1.0 fusion.59
  1317.2 0.9 multiply_reduce_fusion.23
  1320.0 1.9 collective-permute-start.5
  1321.9 100.9 %all-reduce.3 = (f32[]{:T(128)}, f32[]{:T(128)}) all-reduce(f32[]{:T(128)S(6)} %add.349, f32[]{:T(128)S(6)} %add.355), channel_id=1, replica_groups=mesh['hours'=64,'region'=8] {'hours','region'}, use_global_device_ids=true, to_apply=%region_39.40 | all-reduce | flops 2 | bytes 16 | tf_op jit(solution)/shard_map/psum | solution.py:164
  1424.3 24.8 %all_gather.27 = f32[64,1024]{1,0:T(8,128)S(1)} all-gather(f32[64,128]{1,0:T(8,128)S(1)} %get-tuple-element.70), channel_id=1, replica_groups=mesh['hours'=64,'region'=8] {'region'}, dimensions={1}, use_global_device_ids=true | all-gather | bytes 294912 | tf_op jit(solution)/shard_map/all_gather | solution.py:85
  1449.5 1.6 subtract_reduce_fusion
  1451.0 0.7 fusion.69
  1452.1 1.3 fusion.68
  1455.2 32.9 %reduce-scatter.11.cloned.1.call-done = f32[64,128]{1,0:T(8,128)} async-done(((f32[64,1024]{1,0:T(8,128)}), f32[64,128]{1,0:T(8,128)}) %reduce-scatter.11.cloned.1.call-update) | async-done | bytes 32784 | tf_op jit(solution)/shard_map/reduce_scatter | solution.py:144
  1488.1 1.0 fusion.55
  1489.1 0.9 fusion.54
  (86 shorter events, 8.4 us)
Async XLA Ops:
  7.2 465.0 %reduce-scatter.5.cloned.1.call-start = ((), (), s32[]{:S(2)}) async-start(), calls=%async_computation.4 | async-start | bytes 294912 | tf_op jit(solution)/shard_map/reduce_scatter | solution.py:144
  7.9 2.1 copy-start.9
  7.9 461.4 %collective-permute-start = (f32[1,256]{1,0:T(1,128)S(1)}, f32[1,256]{1,0:T(1,128)S(1)}, u32[]{:S(2)}, u32[]{:S(2)}) collective-permute-start(f32[1,256]{1,0:T(1,128)S(1)} %bitcast.122), channel_id=1, source_target_pairs={{0,8},{8,16},{16,24},{24,32},{32,40},{40,48},{48,56},{56,64},{64,7... | collective-permute-start | bytes 3080 | tf_op jit(solution)/shard_map/ppermute | solution.py:14
  36.6 0.7 copy-start.13
  36.6 0.7 copy-start.12
  37.2 0.8 copy-start.1
  37.3 3.8 copy-start
  40.3 853.9 %reduce-scatter.7.cloned.1.call-start = ((), (), s32[]{:S(2)}) async-start(), calls=%async_computation.5 | async-start | bytes 294912 | tf_op jit(solution)/shard_map/reduce_scatter | solution.py:144
  40.3 0.7 copy-start.11
  40.3 0.7 copy-start.5
  40.4 0.7 copy-start.10
  181.0 0.7 copy-start.8
  314.0 11.8 copy-start.3
  340.6 126.1 %copy-start.7 = (f32[256]{0:T(256)S(1)}, f32[256]{0:T(256)}, u32[]{:S(2)}) copy-start(f32[256]{0:T(256)} %param.26) | copy-start | bytes 3076
  469.2 0.7 copy-start.4
  472.1 1.1 copy-start.2
  476.0 262.6 %collective-permute-start.1 = (f32[1,256]{1,0:T(1,128)S(1)}, f32[1,256]{1,0:T(1,128)S(1)}, u32[]{:S(2)}, u32[]{:S(2)}) collective-permute-start(f32[1,256]{1,0:T(1,128)S(1)} %slice.79), channel_id=1, source_target_pairs={{0,504},{8,0},{16,8},{24,16},{32,24},{40,32},{48,40},{56,48},{64,5... | collective-permute-start | bytes 3080 | tf_op jit(solution)/shard_map/ppermute | solution.py:14
  738.6 0.7 copy-start.6
  742.9 573.2 %reduce-scatter.9.cloned.1.call-start = ((), (), s32[]{:S(2)}) async-start(), calls=%async_computation.6 | async-start | bytes 294912 | tf_op jit(solution)/shard_map/reduce_scatter | solution.py:144
  756.0 135.9 %collective-permute-start.2 = (f32[1,256]{1,0:T(1,128)S(1)}, f32[1,256]{1,0:T(1,128)S(1)}, u32[]{:S(2)}, u32[]{:S(2)}) collective-permute-start(f32[1,256]{1,0:T(1,128)S(1)} %slice.80), channel_id=1, source_target_pairs={{0,8},{8,16},{16,24},{24,32},{32,40},{40,48},{48,56},{56,64},{64,7... | collective-permute-start | bytes 3080 | tf_op jit(solution)/shard_map/ppermute | solution.py:14
  898.0 130.7 %collective-permute-start.3 = (f32[1,256]{1,0:T(1,128)S(1)}, f32[1,256]{1,0:T(1,128)S(1)}, u32[]{:S(2)}, u32[]{:S(2)}) collective-permute-start(f32[1,256]{1,0:T(1,128)S(1)} %slice.83), channel_id=1, source_target_pairs={{0,504},{8,0},{16,8},{24,16},{32,24},{40,32},{48,40},{56,48},{64,5... | collective-permute-start | bytes 3080 | tf_op jit(solution)/shard_map/ppermute | solution.py:14
  1161.7 152.2 %collective-permute-start.4 = (f32[1,256]{1,0:T(1,128)S(1)}, f32[1,256]{1,0:T(1,128)S(1)}, u32[]{:S(2)}, u32[]{:S(2)}) collective-permute-start(f32[1,256]{1,0:T(1,128)S(1)} %slice.84), channel_id=1, source_target_pairs={{0,8},{8,16},{16,24},{24,32},{32,40},{40,48},{48,56},{56,64},{64,7... | collective-permute-start | bytes 3080 | tf_op jit(solution)/shard_map/ppermute | solution.py:14
  1166.6 321.5 %reduce-scatter.11.cloned.1.call-start = ((), (), s32[]{:S(2)}) async-start(), calls=%async_computation.7 | async-start | bytes 294912 | tf_op jit(solution)/shard_map/reduce_scatter | solution.py:144
  1320.0 134.3 %collective-permute-start.5 = (f32[1,256]{1,0:T(1,128)S(1)}, f32[1,256]{1,0:T(1,128)S(1)}, u32[]{:S(2)}, u32[]{:S(2)}) collective-permute-start(f32[1,256]{1,0:T(1,128)S(1)} %slice.87), channel_id=1, source_target_pairs={{0,504},{8,0},{16,8},{24,16},{32,24},{40,32},{48,40},{56,48},{64,5... | collective-permute-start | bytes 3080 | tf_op jit(solution)/shard_map/ppermute | solution.py:14
Sparse Core Ops, SparseCore 0:
  40.4 42.1 reduce-scatter.4
  743.0 39.1 reduce-scatter.6
  1166.7 41.5 reduce-scatter.8
  1453.5 34.5 reduce-scatter.10
where the time goes:
time: 1500 us
  blocking collectives  1280 us (85%)
  local copies, waits for them, and re-layouts  86.5 us (6%)
  between operations  36.6 us (2%)
  waiting for transfers between devices  33 us (2%)
  matrix products  26.5 us (2%)
  starting transfers between devices  16.8 us (1%)
  other arithmetic  16.8 us (1%)
    psum x4, blocking collectives, to_owners(): summed = lax.psum(partial_value, 'hours')  515 us
    unnamed x3, blocking collectives  367 us
    psum x3, blocking collectives, body(): dual_sum = lax.psum(dual_sq, ('hours', 'region'))  297 us
    all_gather x4, blocking collectives, body(): lax.all_gather(prices, 'region', axis=1, tiled=True)  101 us
    gather x3, local copies, waits for them, and re-layouts, body(): cap_dense = capacity_all[inverse].reshape(tech_count, node_count)  35.3 us
    gather x3, local copies, waits for them, and re-layouts, body(): jnp.sum(availability * cap_duals, axis=0).reshape(-1)[owner_cols]  35.3 us
    reduce_scatter x4, waiting for transfers between devices, body(): lax.psum_scatter(per_dest, 'region', scatter_dimension=1, tiled=True)  32.9 us
  transfers between devices with their start and end apart: 10, of which 1 were waited for; matrix products, arithmetic and copies ran while one was open for 7% of the time, Pallas kernels for 0%

commit v1 on v0

--- a/solution.py
+++ b/solution.py
@@ -161,7 +161,9 @@
                 + jnp.sum((cap_new - cap_duals) ** 2)
                 + jnp.sum((store_new - store_duals) ** 2)
             )
-            dual_sum = lax.psum(dual_sq, ("hours", "region"))
+            dual_sum = dual_sq
+            for mesh_axis in ("region", "hours"):
+                dual_sum = lax.psum(dual_sum, mesh_axis)
             weight = jnp.sqrt(weight * jnp.sqrt((dual_sum + epsilon) / (primal_sum + epsilon)))
         dispatch, capacity, inner_flow, cross_flow = (
             dispatch_new,

time: 1500 us -> 1570 us (1.047)
  blocking collectives: 1280 us -> 1320 us
  waiting for transfers between devices: 33 us -> 59.9 us
    psum x3 -> x7, blocking collectives: 297 us -> 467 us  [the longest x3 292 us: body(): primal_sum = lax.psum(primal_sq, ('hours', 'region'))]
    psum x4 -> x3, blocking collectives: 515 us -> 373 us  [to_owners(): summed = lax.psum(partial_value, 'hours')]
    reduce_scatter x4, waiting for transfers between devices: 32.9 us -> 59.8 us  [body(): lax.psum_scatter(per_dest, 'region', scatter_dimension=1, tiled=True)]
  transfers between devices with their start and end apart: 10 -> 10, of which waited for: 1 -> 2; matrix products, arithmetic and copies ran while one was open for 7% -> 7% of each run, Pallas kernels for 0% -> 0%
where the time goes in v1:
time: 1570 us
  blocking collectives  1320 us (84%)
  local copies, waits for them, and re-layouts  86.5 us (6%)
  waiting for transfers between devices  59.9 us (4%)
  between operations  36.5 us (2%)
  matrix products  26.5 us (2%)
  starting transfers between devices  21.5 us (1%)
  other arithmetic  16.8 us (1%)
    unnamed x3, blocking collectives  379 us
    psum x3, blocking collectives, to_owners(): summed = lax.psum(partial_value, 'hours')  373 us
    psum x3, blocking collectives, body(): primal_sum = lax.psum(primal_sq, ('hours', 'region'))  292 us
    psum x4, blocking collectives, body(): dual_sum = lax.psum(dual_sum, mesh_axis)  175 us
    all_gather x4, blocking collectives, body(): lax.all_gather(prices, 'region', axis=1, tiled=True)  101 us
    reduce_scatter x4, waiting for transfers between devices, body(): lax.psum_scatter(per_dest, 'region', scatter_dimension=1, tiled=True)  59.8 us
    gather x3, local copies, waits for them, and re-layouts, body(): cap_dense = capacity_all[inverse].reshape(tech_count, node_count)  35.3 us
    gather x3, local copies, waits for them, and re-layouts, body(): jnp.sum(availability * cap_duals, axis=0).reshape(-1)[owner_cols]  35.3 us
  transfers between devices with their start and end apart: 10, of which 2 were waited for; matrix products, arithmetic and copies ran while one was open for 7% of the time, Pallas kernels for 0%

profile of v1, /device:TPU:2, one launch (start us, length us, event | category | flops | bytes accessed | tf_op | source)
XLA Modules:
  0.0 1567.2 jit_solution(8037426835049234256)
XLA Ops:
  7.9 2.0 collective-permute-start
  10.0 26.6 %all_gather.21 = f32[64,1024]{1,0:T(8,128)S(1)} all-gather(f32[64,128]{1,0:T(8,128)} %param.27), channel_id=1, replica_groups=mesh['hours'=64,'region'=8] {'region'}, dimensions={1}, use_global_device_ids=true | all-gather | bytes 294912 | tf_op jit(solution)/shard_map/all_gather | solution.py:85
  37.3 0.7 fusion.75
  38.1 0.9 multiply_reduce_fusion.20
  39.0 1.3 fusion.74
  41.2 11.8 gather_fusion
  53.0 126.8 %psum.91 = f32[2048]{0:T(1024)S(1)} all-reduce(f32[2048]{0:T(1024)S(1)} %gather_fusion), channel_id=1, replica_groups=mesh['hours'=64,'region'=8] {'hours'}, use_global_device_ids=true, to_apply=%region_5.6 | all-reduce | flops 2048 | bytes 16384 | tf_op jit(solution)/shard_map/psum | solution.py:22
  179.7 1.3 dynamic-slice
  181.7 0.7 multiply_reduce_fusion.28
  182.5 126.4 %all-reduce = f32[2048]{0:T(1024)S(1)} all-reduce(f32[2048]{0:T(1024)S(1)} %multiply_dynamic-update-slice_fusion), channel_id=1, replica_groups=mesh['hours'=64,'region'=8] {'hours'}, use_global_device_ids=true, to_apply=%add | all-reduce | flops 2048 | bytes 16384
  308.9 5.0 sort.17
  314.0 11.8 gather_fusion.1
  325.8 1.1 multiply_reduce_fusion.6
  326.8 1.0 multiply_reduce_fusion.21
  328.8 11.8 gather_fusion.2
  343.8 0.9 multiply_reduce_fusion.19
  346.0 6.6 collective-permute-start.1
  352.6 95.6 %psum.94 = f32[]{:T(128)} all-reduce(f32[]{:T(128)S(6)} %add.321), channel_id=1, replica_groups=mesh['hours'=64,'region'=8] {'hours','region'}, use_global_device_ids=true, to_apply=%region_17.18 | all-reduce | flops 1 | bytes 8 | tf_op jit(solution)/shard_map/psum | solution.py:130
  448.2 1.0 fusion.67
  449.3 0.9 multiply_reduce_fusion.25
  452.7 17.2 %psum.92 = f32[]{:T(128)} all-reduce(f32[]{:T(128)S(6)} %add.315), channel_id=1, replica_groups=mesh['hours'=64,'region'=8] {'region'}, use_global_device_ids=true, to_apply=%region_9.10 | all-reduce | flops 1 | bytes 8 | tf_op jit(solution)/shard_map/psum | solution.py:166
  469.9 122.9 %all-reduce.5 = (f32[2048]{0:T(1024)S(1)}, f32[]{:T(128)}) all-reduce(f32[2048]{0:T(1024)S(1)} %gather_fusion.2, f32[]{:T(128)} %psum.92), channel_id=1, replica_groups=mesh['hours'=64,'region'=8] {'hours'}, use_global_device_ids=true, to_apply=%region_22.23 | all-reduce | flops 2049 | bytes 16392 | tf_op jit(solution)/shard_map/psum | solution.py:22
  593.6 25.0 %all_gather.23 = f32[64,1024]{1,0:T(8,128)S(1)} all-gather(f32[64,128]{1,0:T(8,128)S(1)} %get-tuple-element.56), channel_id=1, replica_groups=mesh['hours'=64,'region'=8] {'region'}, dimensions={1}, use_global_device_ids=true | all-gather | bytes 294912 | tf_op jit(solution)/shard_map/all_gather | solution.py:85
  618.6 1.0 multiply_reduce_fusion.17
  620.4 126.1 %all-reduce.1 = f32[2048]{0:T(1024)S(1)} all-reduce(f32[2048]{0:T(1024)S(1)} %subtract_dynamic-update-slice_fusion.1), channel_id=1, replica_groups=mesh['hours'=64,'region'=8] {'hours'}, use_global_device_ids=true, to_apply=%add.1 | all-reduce | flops 2048 | bytes 16384
  746.5 11.8 gather_fusion.3
  759.7 1.9 collective-permute-start.2
  761.6 0.7 fusion.73
  762.3 0.9 multiply_reduce_fusion.16
  763.3 1.3 fusion.72
  764.6 1.2 multiply_reduce_fusion.3
  766.2 11.8 gather_fusion.4
  780.5 1.0 multiply_reduce_fusion.15
  782.8 7.0 collective-permute-start.3
  789.7 98.2 %psum.98 = f32[]{:T(128)} all-reduce(f32[]{:T(128)S(6)} %add.341), channel_id=1, replica_groups=mesh['hours'=64,'region'=8] {'hours','region'}, use_global_device_ids=true, to_apply=%region_33.34 | all-reduce | flops 1 | bytes 8 | tf_op jit(solution)/shard_map/psum | solution.py:130
  888.0 1.0 fusion.63
  889.0 0.9 multiply_reduce_fusion.24
  892.4 17.3 %psum.96 = f32[]{:T(128)} all-reduce(f32[]{:T(128)S(6)} %add.335), channel_id=1, replica_groups=mesh['hours'=64,'region'=8] {'region'}, use_global_device_ids=true, to_apply=%region_25.26 | all-reduce | flops 1 | bytes 8 | tf_op jit(solution)/shard_map/psum | solution.py:166
  909.7 122.9 %all-reduce.4 = (f32[2048]{0:T(1024)S(1)}, f32[]{:T(128)}) all-reduce(f32[2048]{0:T(1024)S(1)} %gather_fusion.4, f32[]{:T(128)} %psum.96), channel_id=1, replica_groups=mesh['hours'=64,'region'=8] {'hours'}, use_global_device_ids=true, to_apply=%region_38.39 | all-reduce | flops 2049 | bytes 16392 | tf_op jit(solution)/shard_map/psum | solution.py:22
  1034.2 1.0 multiply_reduce_fusion.12
  1035.2 24.8 %all_gather.25 = f32[64,1024]{1,0:T(8,128)S(1)} all-gather(f32[64,128]{1,0:T(8,128)S(1)} %get-tuple-element.63), channel_id=1, replica_groups=mesh['hours'=64,'region'=8] {'region'}, dimensions={1}, use_global_device_ids=true | all-gather | bytes 294912 | tf_op jit(solution)/shard_map/all_gather | solution.py:85
  1060.8 126.1 %all-reduce.2 = f32[2048]{0:T(1024)S(1)} all-reduce(f32[2048]{0:T(1024)S(1)} %subtract_dynamic-update-slice_fusion), channel_id=1, replica_groups=mesh['hours'=64,'region'=8] {'hours'}, use_global_device_ids=true, to_apply=%add.2 | all-reduce | flops 2048 | bytes 16384
  1187.0 11.8 gather_fusion.5
  1198.8 1.9 collective-permute-start.4
  1200.7 0.7 fusion.71
  1201.4 0.9 multiply_reduce_fusion.11
  1202.3 1.3 fusion.70
  1203.7 1.4 multiply_reduce_fusion
  1205.5 11.8 gather_fusion.6
  1219.8 0.9 multiply_reduce_fusion.13
  1222.0 22.1 %reduce-scatter.9.cloned.1.call-done = f32[64,128]{1,0:T(8,128)} async-done(((f32[64,1024]{1,0:T(8,128)}), f32[64,128]{1,0:T(8,128)}) %reduce-scatter.9.cloned.1.call-update) | async-done | bytes 32784 | tf_op jit(solution)/shard_map/reduce_scatter | solution.py:144
  1244.1 1.0 fusion.59
  1245.1 0.9 multiply_reduce_fusion.23
  1247.9 1.9 collective-permute-start.5
  1249.9 98.1 %psum.102 = f32[]{:T(128)} all-reduce(f32[]{:T(128)S(6)} %add.361), channel_id=1, replica_groups=mesh['hours'=64,'region'=8] {'hours','region'}, use_global_device_ids=true, to_apply=%region_49.50 | all-reduce | flops 1 | bytes 8 | tf_op jit(solution)/shard_map/psum | solution.py:130
  1348.0 16.5 %psum.100 = f32[]{:T(128)} all-reduce(f32[]{:T(128)S(6)} %add.355), channel_id=1, replica_groups=mesh['hours'=64,'region'=8] {'region'}, use_global_device_ids=true, to_apply=%region_41.42 | all-reduce | flops 1 | bytes 8 | tf_op jit(solution)/shard_map/psum | solution.py:166
  1365.1 124.2 %all-reduce.3 = (f32[]{:T(128)}, f32[2048]{0:T(1024)S(1)}) all-reduce(f32[]{:T(128)} %psum.100, f32[2048]{0:T(1024)S(1)} %gather_fusion.6), channel_id=1, replica_groups=mesh['hours'=64,'region'=8] {'hours'}, use_global_device_ids=true, to_apply=%region_42.43 | all-reduce | flops 2049 | bytes 16392 | tf_op jit(solution)/shard_map/psum | solution.py:166
  1490.1 24.9 %all_gather.27 = f32[64,1024]{1,0:T(8,128)S(1)} all-gather(f32[64,128]{1,0:T(8,128)S(1)} %get-tuple-element.70), channel_id=1, replica_groups=mesh['hours'=64,'region'=8] {'region'}, dimensions={1}, use_global_device_ids=true | all-gather | bytes 294912 | tf_op jit(solution)/shard_map/all_gather | solution.py:85
  1515.4 1.6 subtract_reduce_fusion
  1516.9 0.7 fusion.69
  1518.0 1.3 fusion.68
  1521.1 37.7 %reduce-scatter.11.cloned.1.call-done = f32[64,128]{1,0:T(8,128)} async-done(((f32[64,1024]{1,0:T(8,128)}), f32[64,128]{1,0:T(8,128)}) %reduce-scatter.11.cloned.1.call-update) | async-done | bytes 32784 | tf_op jit(solution)/shard_map/reduce_scatter | solution.py:144
  1558.8 1.0 fusion.55
  1559.8 0.9 fusion.54
  (89 shorter events, 11.1 us)
Async XLA Ops:
  7.2 441.1 %reduce-scatter.5.cloned.1.call-start = ((), (), s32[]{:S(2)}) async-start(), calls=%async_computation.4 | async-start | bytes 294912 | tf_op jit(solution)/shard_map/reduce_scatter | solution.py:144
  7.9 2.1 copy-start.9
  7.9 335.2 %collective-permute-start = (f32[1,256]{1,0:T(1,128)S(1)}, f32[1,256]{1,0:T(1,128)S(1)}, u32[]{:S(2)}, u32[]{:S(2)}) collective-permute-start(f32[1,256]{1,0:T(1,128)S(1)} %bitcast.122), channel_id=1, source_target_pairs={{0,8},{8,16},{16,24},{24,32},{32,40},{40,48},{48,56},{56,64},{64,7... | collective-permute-start | bytes 3080 | tf_op jit(solution)/shard_map/ppermute | solution.py:14
  36.6 0.7 copy-start.13
  36.6 0.7 copy-start.12
  37.2 0.8 copy-start.1
  37.3 3.8 copy-start
  40.3 847.7 %reduce-scatter.7.cloned.1.call-start = ((), (), s32[]{:S(2)}) async-start(), calls=%async_computation.5 | async-start | bytes 294912 | tf_op jit(solution)/shard_map/reduce_scatter | solution.py:144
  40.3 0.7 copy-start.11
  40.3 0.7 copy-start.5
  40.4 0.7 copy-start.10
  181.0 0.7 copy-start.8
  314.0 11.8 copy-start.3
  328.1 0.7 copy-start.7
  343.1 0.7 copy-start.4
  346.0 412.3 %collective-permute-start.1 = (f32[1,256]{1,0:T(1,128)S(1)}, f32[1,256]{1,0:T(1,128)S(1)}, u32[]{:S(2)}, u32[]{:S(2)}) collective-permute-start(f32[1,256]{1,0:T(1,128)S(1)} %slice.79), channel_id=1, source_target_pairs={{0,504},{8,0},{16,8},{24,16},{32,24},{40,32},{48,40},{56,48},{64,5... | collective-permute-start | bytes 3080 | tf_op jit(solution)/shard_map/ppermute | solution.py:14
  448.2 1.0 copy-start.2
  758.3 0.7 copy-start.6
  759.7 20.8 %collective-permute-start.2 = (f32[1,256]{1,0:T(1,128)S(1)}, f32[1,256]{1,0:T(1,128)S(1)}, u32[]{:S(2)}, u32[]{:S(2)}) collective-permute-start(f32[1,256]{1,0:T(1,128)S(1)} %slice.80), channel_id=1, source_target_pairs={{0,8},{8,16},{16,24},{24,32},{32,40},{40,48},{48,56},{56,64},{64,7... | collective-permute-start | bytes 3080 | tf_op jit(solution)/shard_map/ppermute | solution.py:14
  764.6 479.5 %reduce-scatter.9.cloned.1.call-start = ((), (), s32[]{:S(2)}) async-start(), calls=%async_computation.6 | async-start | bytes 294912 | tf_op jit(solution)/shard_map/reduce_scatter | solution.py:144
  782.8 277.3 %collective-permute-start.3 = (f32[1,256]{1,0:T(1,128)S(1)}, f32[1,256]{1,0:T(1,128)S(1)}, u32[]{:S(2)}, u32[]{:S(2)}) collective-permute-start(f32[1,256]{1,0:T(1,128)S(1)} %slice.83), channel_id=1, source_target_pairs={{0,504},{8,0},{16,8},{24,16},{32,24},{40,32},{48,40},{56,48},{64,5... | collective-permute-start | bytes 3080 | tf_op jit(solution)/shard_map/ppermute | solution.py:14
  1198.8 21.0 %collective-permute-start.4 = (f32[1,256]{1,0:T(1,128)S(1)}, f32[1,256]{1,0:T(1,128)S(1)}, u32[]{:S(2)}, u32[]{:S(2)}) collective-permute-start(f32[1,256]{1,0:T(1,128)S(1)} %slice.84), channel_id=1, source_target_pairs={{0,8},{8,16},{16,24},{24,32},{32,40},{40,48},{48,56},{56,64},{64,7... | collective-permute-start | bytes 3080 | tf_op jit(solution)/shard_map/ppermute | solution.py:14
  1203.7 355.2 %reduce-scatter.11.cloned.1.call-start = ((), (), s32[]{:S(2)}) async-start(), calls=%async_computation.7 | async-start | bytes 294912 | tf_op jit(solution)/shard_map/reduce_scatter | solution.py:144
  1247.9 272.3 %collective-permute-start.5 = (f32[1,256]{1,0:T(1,128)S(1)}, f32[1,256]{1,0:T(1,128)S(1)}, u32[]{:S(2)}, u32[]{:S(2)}) collective-permute-start(f32[1,256]{1,0:T(1,128)S(1)} %slice.87), channel_id=1, source_target_pairs={{0,504},{8,0},{16,8},{24,16},{32,24},{40,32},{48,40},{56,48},{64,5... | collective-permute-start | bytes 3080 | tf_op jit(solution)/shard_map/ppermute | solution.py:14
Sparse Core Ops, SparseCore 0:
  40.4 42.1 reduce-scatter.4
  764.7 39.7 reduce-scatter.6
  1203.8 40.2 reduce-scatter.8
  1519.4 39.3 reduce-scatter.10
